TPU v7x, 32 devices: a whole 2x2x4 slice. The times are simulated.
32 devices in a mesh: node: 8 (over y, x, core), batch: 4 (over z).
Axes of the slice: x: 2, y: 2, z: 4, core: 2. Of those that a mesh axis runs over, the one named last changes fastest.
Arguments:
- memory: bfloat16 [65536, 128], P('node'), may hold values from -5 to 5
- src_owner: int32 [16384, 1], P(('node', 'batch')), may hold values from 0 to 7; in each aligned block of 512 rows (0 to 511, 512 to 1023, ...) at most 128 rows name the same one
- src_row: int32 [16384], P(('node', 'batch')), may hold values from 0 to 8191
- fetch_owner: int32 [16384, 11, 1], P(('node', 'batch')), may hold values from 0 to 7; in each aligned block of 5632 rows (0 to 5631, 5632 to 11263, ..., all dimensions but the last counted through in order) at most 1408 rows name the same one
- fetch_row: int32 [16384, 11], P(('node', 'batch')), may hold values from 0 to 8191
- event_tick: int32 [16384], P(('node', 'batch')), may hold values from 5000 to 9999
- source_tick: int32 [16384], P(('node', 'batch')), may hold values from 0 to 4999
- neighbour_tick: int32 [16384, 10], P(('node', 'batch')), may hold values from 0 to 4999
- time_freq: float32 [128], replicated, may hold values from 0.0001 to 0.1
- time_phase: float32 [128], replicated, may hold values from -3.140625 to 3.140625
- gru_input: bfloat16 [256, 384], replicated, may hold values from -0.375 to 0.375
- gru_hidden: bfloat16 [128, 384], replicated, may hold values from -0.5 to 0.5
- gru_bias: float32 [512], replicated, may hold values from -3 to 3
- w_query: bfloat16 [128, 128], replicated, may hold values from -0.5 to 0.5
- w_kv: bfloat16 [256, 256], replicated, may hold values from -0.375 to 0.375
- w_merge: bfloat16 [256, 128], replicated, may hold values from -0.375 to 0.375
- merge_bias: float32 [128], replicated, may hold values from -3 to 3
- out_grad: float32 [16384, 128], P(('node', 'batch')), may hold values from -0.02 to 0.02
Outputs:
- embedding: float32 [16384, 128], P(('node', 'batch'))
- memory_out: bfloat16 [65536, 128], P('node')
- grad_query: float32 [128, 128], replicated
- grad_kv: float32 [256, 256], replicated
- grad_merge: float32 [256, 128], replicated
- grad_bias: float32 [128], replicated
Inputs may be any that keep to these rules, and one draw needn't show every extreme that they name: `src_owner`: among the 512 events of one device no owner is named by more than 128 of them. `fetch_owner`: among the 512 * (11) entries of one device no owner is named by more than 1408 of them.
All inputs are finite; a program needn't handle non-finite values.
Results may differ from a plain program's by a relative error of at most 0.012.
Values may be sent and summed in bfloat16 or wider, within the bound.
A program may use at most 64 MiB of HBM per device.

v0:
```python
import math
import jax
import jax.numpy as jnp
from jax import lax
from jax.sharding import PartitionSpec as P

HEADS = 2


def time_code(delta, freq, phase):
    return jnp.cos(delta[..., None] * freq + phase)


def gru_cell(message, state, gru_input, gru_hidden, gru_bias):
    width = state.shape[-1]
    from_msg = (
        jnp.dot(message, gru_input, preferred_element_type=jnp.float32) + gru_bias[: 3 * width]
    )
    from_state = jnp.dot(state, gru_hidden, preferred_element_type=jnp.float32)
    reset = jax.nn.sigmoid(from_msg[:, :width] + from_state[:, :width])
    update = jax.nn.sigmoid(from_msg[:, width : 2 * width] + from_state[:, width : 2 * width])
    candid = jnp.tanh(
        from_msg[:, 2 * width :] + reset * (from_state[:, 2 * width :] + gru_bias[3 * width :])
    )
    return ((1.0 - update) * candid + update * state.astype(jnp.float32)).astype(jnp.bfloat16)


def last_pick(owner_ids, row_ids):
    same = (owner_ids[:, None] == owner_ids[None, :]) & (row_ids[:, None] == row_ids[None, :])
    places = jnp.arange(owner_ids.shape[0], dtype=jnp.int32)
    return jnp.max(jnp.where(same, places[None, :], jnp.int32(-1)), axis=1)


def place(owner_ids, owner_count, capacity):
    onehot = (owner_ids[:, None] == jnp.arange(owner_count, dtype=jnp.int32)[None, :]).astype(
        jnp.int32
    )
    before = jnp.cumsum(onehot, axis=0) - onehot
    return owner_ids * capacity + jnp.sum(before * onehot, axis=1)


def embed(query_w, pair_w, merge_w, bias_term, new_src, kv_in):
    att_width = query_w.shape[1]
    head_width = att_width // HEADS
    row_count = new_src.shape[0]
    nb_count = kv_in.shape[1]
    query_rows = jnp.dot(new_src, query_w.astype(jnp.bfloat16), preferred_element_type=jnp.float32)
    pairs = jnp.dot(kv_in, pair_w.astype(jnp.bfloat16), preferred_element_type=jnp.float32)
    key_rows = pairs[..., :att_width].reshape(row_count, nb_count, HEADS, head_width)
    value_rows = pairs[..., att_width:].reshape(row_count, nb_count, HEADS, head_width)
    scores = jnp.einsum(
        "ehd,enhd->ehn", query_rows.reshape(row_count, HEADS, head_width), key_rows
    ) / math.sqrt(head_width)
    scores = scores - jnp.max(scores, axis=-1, keepdims=True)
    shares = jnp.exp(scores)
    shares = shares / jnp.sum(shares, axis=-1, keepdims=True)
    mixed = (
        jnp.einsum("ehn,enhd->ehd", shares, value_rows)
        .reshape(row_count, att_width)
        .astype(jnp.bfloat16)
    )
    joined = jnp.concatenate([mixed, new_src], axis=-1)
    return jax.nn.silu(
        jnp.dot(joined, merge_w.astype(jnp.bfloat16), preferred_element_type=jnp.float32)
        + bias_term
    )


def on_device(
    memory,
    src_owner,
    src_row,
    fetch_owner,
    fetch_row,
    event_tick,
    source_tick,
    neighbour_tick,
    time_freq,
    time_phase,
    gru_input,
    gru_hidden,
    gru_bias,
    w_query,
    w_kv,
    w_merge,
    merge_bias,
    out_grad,
):
    owner_count = lax.axis_size("node")
    batch_count = lax.axis_size("batch")
    batch_place = lax.axis_index("batch")
    event_count = src_row.shape[0]
    per_event = fetch_row.shape[1]
    mem_width = memory.shape[1]
    node_local = memory.shape[0]
    far_cap = event_count * per_event * 2 // owner_count
    near_cap = event_count * 2 // owner_count
    near_owner = src_owner[:, 0]
    far_slot = place(fetch_owner.reshape(-1), owner_count, far_cap)
    near_slot = place(near_owner, owner_count, near_cap)
    far_ask = (
        jnp.zeros((owner_count * far_cap,), jnp.int32)
        .at[far_slot]
        .set(fetch_row.reshape(-1))
        .reshape(owner_count, far_cap)
    )
    near_ask = (
        jnp.zeros((owner_count * near_cap,), jnp.int32)
        .at[near_slot]
        .set(src_row + 1)
        .reshape(owner_count, near_cap)
    )
    far_got, near_got = (
        lax.all_to_all(far_ask, "node", split_axis=0, concat_axis=0, tiled=True),
        lax.all_to_all(near_ask, "node", split_axis=0, concat_axis=0, tiled=True),
    )
    near_flat = near_got.reshape(-1)
    near_live = near_flat > 0
    near_index = jnp.maximum(near_flat - 1, 0)
    far_rows = memory[far_got]
    near_rows = memory[near_index].reshape(owner_count, near_cap, mem_width)
    source_code = time_code(
        (event_tick - source_tick).astype(jnp.float32), time_freq, time_phase
    ).astype(jnp.bfloat16)
    far_back = lax.all_to_all(far_rows, "node", split_axis=0, concat_axis=0, tiled=True)
    fetched = far_back.reshape(owner_count * far_cap, mem_width)[far_slot].reshape(
        event_count, per_event, mem_width
    )
    message = jnp.concatenate([fetched[:, 0], source_code], axis=-1)
    msg_width = message.shape[1]
    outgoing = (
        jnp.zeros((owner_count * near_cap, msg_width), jnp.bfloat16)
        .at[near_slot]
        .set(message)
        .reshape(owner_count, near_cap, msg_width)
    )
    arrived = lax.all_to_all(outgoing, "node", split_axis=0, concat_axis=0, tiled=True)
    fresh = gru_cell(
        arrived.reshape(-1, msg_width),
        near_rows.reshape(-1, mem_width),
        gru_input,
        gru_hidden,
        gru_bias,
    )
    returned = lax.all_to_all(
        fresh.reshape(owner_count, near_cap, mem_width),
        "node",
        split_axis=0,
        concat_axis=0,
        tiled=True,
    )
    updated = returned.reshape(owner_count * near_cap, mem_width)[near_slot]
    sender_ids = jnp.repeat(jnp.arange(owner_count, dtype=jnp.int32), near_cap)
    slot_ids = jnp.tile(jnp.arange(near_cap, dtype=jnp.int32), owner_count)
    priority = (sender_ids * batch_count + batch_place) * near_cap + slot_ids
    packed = jnp.where(near_live, priority * node_local + near_index, jnp.int32(-1))
    all_fresh, all_keys = (
        lax.all_gather(fresh, "batch", axis=0, tiled=True),
        lax.all_gather(packed, "batch", axis=0, tiled=True),
    )
    key_live = all_keys >= 0
    key_rows = jnp.where(key_live, all_keys % node_local, node_local).astype(jnp.int32)
    best = jnp.full((node_local + 1,), -1, jnp.int32).at[key_rows].max(all_keys)
    winner = key_live & (all_keys == best[key_rows])
    target = jnp.where(winner, key_rows, node_local)
    memory_out = memory.at[target].set(all_fresh, mode="drop")
    new_src = updated[last_pick(near_owner, src_row)]
    nb_code = time_code(
        (event_tick[:, None] - neighbour_tick).astype(jnp.float32), time_freq, time_phase
    ).astype(jnp.bfloat16)
    kv_in = jnp.concatenate([fetched[:, 1:], nb_code], axis=-1)

    def forward(query_w, pair_w, merge_w, bias_term):
        return embed(query_w, pair_w, merge_w, bias_term, new_src, kv_in)

    result, pull = jax.vjp(
        forward,
        w_query.astype(jnp.float32),
        w_kv.astype(jnp.float32),
        w_merge.astype(jnp.float32),
        merge_bias,
    )
    grads = pull(out_grad)
    summed = lax.psum((grads[0], grads[1], grads[2], grads[3]), ("node", "batch"))
    return (result, memory_out, summed[0], summed[1], summed[2], summed[3])


def solution(mesh):
    return jax.shard_map(
        on_device,
        mesh=mesh,
        in_specs=(
            P("node", None),
            P(("node", "batch"), None),
            P(("node", "batch")),
            P(("node", "batch"), None, None),
            P(("node", "batch"), None),
            P(("node", "batch")),
            P(("node", "batch")),
            P(("node", "batch"), None),
            P(),
            P(),
            P(),
            P(),
            P(),
            P(),
            P(),
            P(),
            P(),
            P(("node", "batch"), None),
        ),
        out_specs=(P(("node", "batch"), None), P("node", None), P(), P(), P(), P()),
        check_vma=False,
    )
```

profile of v0, /device:TPU:1, one launch (start us, length us, event | category | flops | bytes accessed | tf_op | source)
XLA Modules:
  0.0 348.3 jit_solution(14605585450725997113)
XLA Ops:
  8.0 1.6 copy.109
  10.7 2.4 reduce-window.16
  14.3 21.1 %scatter_custom_fusion = s32[11264]{0:T(1024)S(1)} fusion(s32[5632]{0:T(1024)S(1)} %fusion.43, s32[5632]{0:T(1024)S(1)} %reshape.304, s32[]{:T(128)} %constant.24.clone.1), kind=kCustom, calls=%fused_computation.91 | custom fusion | bytes 45060 | tf_op jit(solution)/shard_map/scatter | solution.py:104
  35.4 9.1 %all_to_all.36 = s32[8,1,1408]{2,1,0:T(1,128)S(1)} all-to-all(s32[8,1,1408]{2,1,0:T(1,128)S(1)} %bitcast.125), channel_id=1, replica_groups=mesh['node'=8,'batch'=4] {'node'}, dimensions={0} | all-to-all | bytes 90112 | tf_op jit(solution)/shard_map/all_to_all | solution.py:114
  44.6 39.8 %gather_fusion = bf16[11264,128]{1,0:T(8,128)(2,1)} fusion(bf16[8192,128]{1,0:T(8,128)(2,1)S(1)} %copy.109, s32[11264]{0:T(1024)S(1)} %broadcast_clamp_fusion), kind=kCustom, calls=%fused_computation | custom fusion | bytes 5812224 | tf_op jit(solution)/shard_map/gather | solution.py:120
  84.5 5.3 %all-to-all-start.1 = ((bf16[8,1408,128]{2,1,0:T(8,128)(2,1)}), bf16[8,1408,128]{2,1,0:T(8,128)(2,1)}, u32[]{:S(2)}, u32[]{:S(2)}) async-start(bf16[8,1408,128]{2,1,0:T(8,128)(2,1)} %bitcast.114), calls=%async_computation.1 | async-start | bytes 5767168 | tf_op jit(solution)/shard_map/all_to_all | solution.py:125
  89.8 1.1 reduce-window.14
  91.3 3.0 scatter_custom_fusion.2
  94.3 0.4 select_reduce_fusion
  94.8 0.9 cosine_convert_fusion.1
  95.7 10.1 %cosine_convert_fusion = bf16[512,10,128]{2,0,1:T(8,128)(2,1)} fusion(f32[128]{0:T(128)S(1)} %copy-done.17, f32[128]{0:T(128)S(1)} %copy-done.18, f32[512,10]{0,1:T(8,128)S(1)} %subtract_convert_fusion), kind=kLoop, calls=%fused_computation.20 | loop fusion | flops 1966080 | bytes 1332224 | tf_op jit(solution)/shard_map/convert_element_type | solution.py:170
  105.8 15.5 %all-to-all-done.1 = bf16[8,1408,128]{2,1,0:T(8,128)(2,1)} async-done(((bf16[8,1408,128]{2,1,0:T(8,128)(2,1)}), bf16[8,1408,128]{2,1,0:T(8,128)(2,1)}, u32[]{:S(2)}, u32[]{:S(2)}) %all-to-all-start.1) | async-done | bytes 2883616 | tf_op jit(solution)/shard_map/all_to_all | solution.py:125
  121.3 6.9 %all-to-all-start.3 = ((s32[8,1,128]{2,1,0:T(1,128)}), s32[8,1,128]{2,1,0:T(1,128)S(1)}, u32[]{:S(2)}, u32[]{:S(2)}) async-start(s32[8,1,128]{2,1,0:T(1,128)} %bitcast.18), calls=%async_computation.3 | async-start | bytes 8192 | tf_op jit(solution)/shard_map/all_to_all | solution.py:115
  128.2 13.4 %gather_fusion.1 = bf16[5632,128]{1,0:T(8,128)(2,1)} fusion(bf16[11264,128]{1,0:T(8,128)(2,1)} %bitcast.15, s32[6144]{0:T(1024)S(1)} %pad_clamp_fusion), kind=kCustom, calls=%fused_computation.1 | custom fusion | bytes 2906112 | tf_op jit(solution)/shard_map/gather | solution.py:126
  141.6 3.7 %reshape.238 = bf16[512,11,128]{2,1,0:T(8,128)(2,1)} reshape(bf16[5632,128]{1,0:T(8,128)(2,1)} %gather_fusion.1) | data formatting | bytes 2883584 | tf_op jit(solution)/shard_map/reshape | solution.py:126
  145.3 1.4 slice.78
  146.7 3.2 scatter_custom_fusion.1
  149.9 4.2 %all-to-all-start.2 = ((bf16[8,128,256]{2,1,0:T(8,128)(2,1)}), bf16[8,128,256]{2,1,0:T(8,128)(2,1)S(1)}, u32[]{:S(2)}, u32[]{:S(2)}) async-start(bf16[8,128,256]{2,1,0:T(8,128)(2,1)} %bitcast.16), calls=%async_computation.2 | async-start | bytes 1048576 | tf_op jit(solution)/shard_map/all_to_all | solution.py:137
  154.1 3.2 gather_fusion.2
  157.3 10.6 %all_gather.6 = s32[4096]{0:T(1024)S(1)} all-gather(s32[1024]{0:T(1024)S(1)} %get-tuple-element.24), channel_id=1, replica_groups=mesh['node'=8,'batch'=4] {'batch'}, dimensions={0}, use_global_device_ids=true | all-gather | bytes 20480 | tf_op jit(solution)/shard_map/all_gather | solution.py:159
  168.0 1.5 fusion.65
  169.5 2.6 slice.85
  172.0 1.4 copy.95
  173.4 0.4 convolution_add_fusion
  173.9 1.0 copy-done.4
  174.8 1.1 fusion.21
  175.9 7.1 %all-to-all-start.4 = ((bf16[8,128,128]{2,1,0:T(8,128)(2,1)}), bf16[8,128,128]{2,1,0:T(8,128)(2,1)S(1)}, u32[]{:S(2)}, u32[]{:S(2)}) async-start(bf16[8,128,128]{2,1,0:T(8,128)(2,1)} %bitcast.21), calls=%async_computation.4 | async-start | bytes 524288 | tf_op jit(solution)/shard_map/all_to_all | solution.py:145
  183.0 2.6 fusion.4
  185.6 2.3 copy-done.2
  188.0 0.6 all-to-all-done.4
  188.6 1.3 gather_fusion.3
  189.9 1.3 gather_fusion.4
  191.5 4.0 %multiply_reduce_fusion.3 = (f32[512,2,10]{0,1,2:T(2,128)S(1)}, f32[512,10,128]{0,2,1:T(8,128)}) fusion(f32[512,2,64]{0,2,1:T(8,128)S(1)} %bitcast.119, f32[512,10,256]{0,2,1:T(8,128)} %copy-done.2), kind=kLoop, calls=%fused_computation.19 | loop fusion | flops 1300480 | bytes 5545984 | tf_op jit(solution)/shard_map/jvp(ehd,enhd->ehn)/dot_general | solution.py:51
  196.6 1.0 fusion.62
  197.8 2.6 broadcast_multiply_fusion.1
  200.6 0.9 fusion.14
  201.6 0.4 broadcast_multiply_fusion
  202.0 0.9 fusion.15
  202.9 0.4 copy-done.6
  203.3 1.6 fusion.11
  204.9 24.3 %scatter_custom_fusion.3 = s32[8193]{0:T(1024)S(1)} fusion(s32[4096]{0:T(1024)S(1)} %get-tuple-element.23, s32[4096]{0:T(1024)S(1)} %all_gather.6, s32[]{:T(128)} %constant.30.clone.1), kind=kCustom, calls=%fused_computation.96 | custom fusion | flops 4096 | bytes 32776 | tf_op jit(solution)/shard_map/scatter-max | solution.py:163
  229.2 23.0 %gather_fusion.5 = s32[4096]{0:T(1024)S(1)} fusion(s32[8193]{0:T(1024)S(1)} %scatter_custom_fusion.3, s32[4096]{0:T(1024)S(1)} %get-tuple-element.22), kind=kCustom, calls=%fused_computation.5 | custom fusion | bytes 49152 | tf_op jit(solution)/shard_map/gather | solution.py:164
  252.3 41.2 %psum.31 = f32[128]{0:T(128)} all-reduce(f32[128]{0:T(128)S(1)} %get-tuple-element.11), channel_id=1, replica_groups=mesh['node'=8,'batch'=4] {'node','batch'}, use_global_device_ids=true, to_apply=%region_21.22 | all-reduce | flops 128 | bytes 1024 | tf_op jit(solution)/shard_map/psum | solution.py:184
  293.5 12.5 %scatter_fusion = bf16[8192,128]{1,0:T(8,128)(2,1)S(1)} fusion(bf16[8192,128]{1,0:T(8,128)(2,1)S(1)} %copy.109, s32[4096]{0:T(1024)S(1)} %compare_select_fusion.2, bf16[4096,128]{1,0:T(8,128)(2,1)} %all-gather.2.cloned.1.call-done), kind=kCustom, calls=%fused_computation.10 | custom fusion | bytes 3162112 | tf_op jit(solution)/shard_map/scatter | solution.py:166
  306.0 30.2 %all-reduce.5.cloned.1.call-done = (f32[128,128]{1,0:T(8,128)}, f32[256,256]{1,0:T(8,128)}, f32[256,128]{1,0:T(8,128)}) async-done(((f32[128,128]{1,0:T(8,128)}, f32[256,256]{1,0:T(8,128)}, f32[256,128]{1,0:T(8,128)}), (f32[128,128]{1,0:T(8,128)}, f32[256,256]{1,0:T(8,128)}, f32[256,128]{1,0:T(8,128)})) %all-reduce.5.cloned.1.call-update) | async-done | bytes 458768 | tf_op jit(solution)/shard_map/psum | solution.py:184
  336.2 1.5 copy.110
  337.6 1.7 copy.111
  339.3 1.6 copy.112
  (100 shorter events, 4.5 us)
Async XLA Ops:
  8.0 165.4 %copy-start = (bf16[256,384]{1,0:T(8,128)(2,1)S(1)}, bf16[256,384]{1,0:T(8,128)(2,1)}, u32[]{:S(2)}) copy-start(bf16[256,384]{1,0:T(8,128)(2,1)} %param.28) | copy-start | bytes 589828
  8.0 1.7 copy-start.9
  8.0 5.7 %copy-start.12 = (s32[512,11]{0,1:T(8,128)S(1)}, s32[512,11]{0,1:T(8,128)}, u32[]{:S(2)}) copy-start(s32[512,11]{0,1:T(8,128)} %param.22) | copy-start | bytes 67588
  84.4 5.3 %copy-start.11 = (s32[512,1]{0,1:T(1,128)S(1)}, s32[512,1]{0,1:T(1,128)}, u32[]{:S(2)}) copy-start(s32[512,1]{0,1:T(1,128)} %param.19) | copy-start | bytes 6148
  84.4 6.8 %copy-start.15 = (s32[512]{0:T(512)S(1)}, s32[512]{0:T(512)}, u32[]{:S(2)}) copy-start(s32[512]{0:T(512)} %param.20) | copy-start | bytes 6148
  84.4 10.3 %copy-start.16 = (s32[512]{0:T(512)S(1)}, s32[512]{0:T(512)}, u32[]{:S(2)}) copy-start(s32[512]{0:T(512)} %param.23) | copy-start | bytes 6148
  84.4 10.3 %copy-start.19 = (s32[512]{0:T(512)S(1)}, s32[512]{0:T(512)}, u32[]{:S(2)}) copy-start(s32[512]{0:T(512)} %param.24) | copy-start | bytes 6148
  84.4 10.3 %copy-start.13 = (s32[512,10]{0,1:T(8,128)S(1)}, s32[512,10]{0,1:T(8,128)}, u32[]{:S(2)}) copy-start(s32[512,10]{0,1:T(8,128)} %param.25) | copy-start | bytes 61444
  84.5 10.3 %copy-start.17 = (f32[128]{0:T(128)S(1)}, f32[128]{0:T(128)}, u32[]{:S(2)}) copy-start(f32[128]{0:T(128)} %param.27) | copy-start | bytes 1540
  84.5 10.3 %copy-start.18 = (f32[128]{0:T(128)S(1)}, f32[128]{0:T(128)}, u32[]{:S(2)}) copy-start(f32[128]{0:T(128)} %param.26) | copy-start | bytes 1540
  84.5 43.7 %copy-start.20 = (f32[512]{0:T(512)S(1)}, f32[512]{0:T(512)}, u32[]{:S(2)}) copy-start(f32[512]{0:T(512)} %param.30) | copy-start | bytes 6148
  84.5 36.8 %all-to-all-start.1 = ((bf16[8,1408,128]{2,1,0:T(8,128)(2,1)}), bf16[8,1408,128]{2,1,0:T(8,128)(2,1)}, u32[]{:S(2)}, u32[]{:S(2)}) async-start(bf16[8,1408,128]{2,1,0:T(8,128)(2,1)} %bitcast.114), calls=%async_computation.1 | async-start | bytes 5767168 | tf_op jit(solution)/shard_map/all_to_all | solution.py:125
  121.3 28.5 %all-to-all-start.3 = ((s32[8,1,128]{2,1,0:T(1,128)}), s32[8,1,128]{2,1,0:T(1,128)S(1)}, u32[]{:S(2)}, u32[]{:S(2)}) async-start(s32[8,1,128]{2,1,0:T(1,128)} %bitcast.18), calls=%async_computation.3 | async-start | bytes 8192 | tf_op jit(solution)/shard_map/all_to_all | solution.py:115
  145.3 22.7 %copy-start.8 = (bf16[128,384]{1,0:T(8,128)(2,1)S(1)}, bf16[128,384]{1,0:T(8,128)(2,1)}, u32[]{:S(2)}) copy-start(bf16[128,384]{1,0:T(8,128)(2,1)} %param.29) | copy-start | bytes 294916
  149.9 23.6 %all-to-all-start.2 = ((bf16[8,128,256]{2,1,0:T(8,128)(2,1)}), bf16[8,128,256]{2,1,0:T(8,128)(2,1)S(1)}, u32[]{:S(2)}, u32[]{:S(2)}) async-start(bf16[8,128,256]{2,1,0:T(8,128)(2,1)} %bitcast.16), calls=%async_computation.2 | async-start | bytes 1048576 | tf_op jit(solution)/shard_map/all_to_all | solution.py:137
  173.4 1.4 copy-start.4
  174.8 8.2 %copy-start.7 = (bf16[256,256]{1,0:T(8,128)(2,1)S(1)}, bf16[256,256]{1,0:T(8,128)(2,1)}, u32[]{:S(2)}) copy-start(bf16[256,256]{1,0:T(8,128)(2,1)} %param.32) | copy-start | bytes 393220
  175.9 12.7 %all-to-all-start.4 = ((bf16[8,128,128]{2,1,0:T(8,128)(2,1)}), bf16[8,128,128]{2,1,0:T(8,128)(2,1)S(1)}, u32[]{:S(2)}, u32[]{:S(2)}) async-start(bf16[8,128,128]{2,1,0:T(8,128)(2,1)} %bitcast.21), calls=%async_computation.4 | async-start | bytes 524288 | tf_op jit(solution)/shard_map/all_to_all | solution.py:145
  183.0 110.5 %all-gather.2.cloned.1.call-start = ((), (), s32[]{:S(2)}) async-start(), calls=%async_computation.5 | async-start | bytes 1310720 | tf_op jit(solution)/shard_map/all_gather | solution.py:158
  185.6 2.3 copy-start.2
  187.9 3.4 copy-start.14
  187.9 148.2 %all-reduce.5.cloned.1.call-start = ((), (), s32[]{:S(2)}) async-start(), calls=%async_computation.6 | async-start | bytes 917504 | tf_op jit(solution)/shard_map/psum | solution.py:184
  191.5 4.2 %slice-start = ((f32[512,10,256]{0,2,1:T(8,128)}), f32[512,10,128]{0,2,1:T(8,128)S(1)}, s32[]{:S(2)}) async-start(f32[512,10,256]{0,2,1:T(8,128)} %copy-done.2), calls=%async_computation.7 | async-start | bytes 5242880 | tf_op jit(solution)/shard_map/jvp()/slice | solution.py:50
  195.6 0.8 copy-start.10
  195.6 1.0 copy-start.21
  195.6 1.0 copy-start.22
  197.8 3.7 %copy-start.3 = (f32[512,10,128]{0,2,1:T(8,128)S(1)}, f32[512,10,128]{0,2,1:T(8,128)}, u32[]{:S(2)}) copy-start(f32[512,10,128]{0,2,1:T(8,128)} %get-tuple-element.16) | copy-start | bytes 7864324
  201.6 1.3 copy-start.5
  201.6 1.7 copy-start.6
  306.0 34.9 %copy-start.1 = (bf16[8192,128]{1,0:T(8,128)(2,1)}, bf16[8192,128]{1,0:T(8,128)(2,1)S(1)}, u32[]{:S(2)}) copy-start(bf16[8192,128]{1,0:T(8,128)(2,1)S(1)} %scatter_fusion) | copy-start | bytes 6291460
Sparse Core Ops, SparseCore 0:
  188.1 28.9 all-gather.1
Sparse Core Ops, SparseCore 1:
  205.0 131.1 all-reduce.4
where the time goes:
time: 349 us; the launch traced here: 348 us
  local copies, waits for them, and re-layouts  140 us (40%)
  blocking collectives  60.9 us (17%)
  other arithmetic  51.9 us (15%)
  waiting for transfers between devices  46.4 us (13%)
  starting transfers between devices  23.5 us (7%)
  between operations  16 us (5%)
  matrix products  9.36 us (3%)
    psum x1, blocking collectives, on_device(): lax.psum((grads[0], grads[1], grads[2], grads[3]), ('node', 'batch'))  41.2 us
    gather x1, local copies, waits for them, and re-layouts, on_device(): far_rows = memory[far_got]  39.8 us
    psum x1, waiting for transfers between devices, on_device(): lax.psum((grads[0], grads[1], grads[2], grads[3]), ('node', 'batch'))  30.2 us
    another operation x1, other arithmetic, on_device(): best = jnp.full((node_local + 1,), -1, jnp.int32).at[key_rows].max(all_keys)  24.3 us
    gather x1, local copies, waits for them, and re-layouts, on_device(): winner = key_live & (all_keys == best[key_rows])  23 us
    scatter x1, local copies, waits for them, and re-layouts, on_device(): far_ask = jnp.zeros((owner_count * far_cap,), jnp.int32).at[far_slot].set...  21.1 us
    all_to_all x1, waiting for transfers between devices, on_device(): lax.all_to_all(far_rows, 'node', split_axis=0, concat_axis=0, tiled=True)  15.5 us
    gather x1, local copies, waits for them, and re-layouts, on_device(): far_back.reshape(owner_count * far_cap, mem_width)[far_slot]  13.4 us
  transfers between devices with their start and end apart: 6, of which 3 were waited for; matrix products, arithmetic and copies ran while one was open for 36% of the time, Pallas kernels for 0%

commit v1 on v0

--- a/solution.py
+++ b/solution.py
@@ -181,7 +181,9 @@
         merge_bias,
     )
     grads = pull(out_grad)
-    summed = lax.psum((grads[0], grads[1], grads[2], grads[3]), ("node", "batch"))
+    z_in = (grads[0], grads[1], grads[2], grads[3])
+    back = lax.psum(z_in, "batch")
+    summed = lax.psum(back, "node")
     return (result, memory_out, summed[0], summed[1], summed[2], summed[3])
 
 

time: 349 us -> 330 us (0.946)
  blocking collectives: 60.9 us -> 45.3 us
    psum x1 -> x2, blocking collectives: 41.2 us -> 25.6 us  [the longest x1 17.4 us: on_device(): summed = lax.psum(back, 'node')]
    psum x1 -> x2, waiting for transfers between devices: 30.2 us -> 29.1 us  [the longest x1 26.3 us: on_device(): back = lax.psum(z_in, 'batch')]
  transfers between devices with their start and end apart: 6 -> 7, of which waited for: 3 -> 4; matrix products, arithmetic and copies ran while one was open for 36% -> 33% of each run, Pallas kernels for 0% -> 0%
where the time goes in v1:
time: 330 us; the launch traced here: 328 us
  local copies, waits for them, and re-layouts  140 us (42%)
  other arithmetic  51.9 us (16%)
  waiting for transfers between devices  46.1 us (14%)
  blocking collectives  45.3 us (14%)
  starting transfers between devices  20.8 us (6%)
  between operations  14.3 us (4%)
  matrix products  9.36 us (3%)
    gather x1, local copies, waits for them, and re-layouts, on_device(): far_rows = memory[far_got]  39.8 us
    psum x1, waiting for transfers between devices, on_device(): back = lax.psum(z_in, 'batch')  26.3 us
    another operation x1, other arithmetic, on_device(): best = jnp.full((node_local + 1,), -1, jnp.int32).at[key_rows].max(all_keys)  24.3 us
    gather x1, local copies, waits for them, and re-layouts, on_device(): winner = key_live & (all_keys == best[key_rows])  23 us
    scatter x1, local copies, waits for them, and re-layouts, on_device(): far_ask = jnp.zeros((owner_count * far_cap,), jnp.int32).at[far_slot].set...  21.1 us
    psum x1, blocking collectives, on_device(): summed = lax.psum(back, 'node')  17.4 us
    all_to_all x1, waiting for transfers between devices, on_device(): lax.all_to_all(far_rows, 'node', split_axis=0, concat_axis=0, tiled=True)  15.5 us
    gather x1, local copies, waits for them, and re-layouts, on_device(): far_back.reshape(owner_count * far_cap, mem_width)[far_slot]  13.4 us
  transfers between devices with their start and end apart: 7, of which 4 were waited for; matrix products, arithmetic and copies ran while one was open for 33% of the time, Pallas kernels for 0%

profile of v1, /device:TPU:1, one launch (start us, length us, event | category | flops | bytes accessed | tf_op | source)
XLA Modules:
  0.0 328.0 jit_solution(12235207125847414358)
XLA Ops:
  7.2 1.6 copy.112
  9.9 2.4 reduce-window.16
  13.4 21.1 %scatter_custom_fusion = s32[11264]{0:T(1024)S(1)} fusion(s32[5632]{0:T(1024)S(1)} %fusion.43, s32[5632]{0:T(1024)S(1)} %reshape.304, s32[]{:T(128)} %constant.24.clone.1), kind=kCustom, calls=%fused_computation.91 | custom fusion | bytes 45060 | tf_op jit(solution)/shard_map/scatter | solution.py:104
  34.6 9.1 %all_to_all.36 = s32[8,1,1408]{2,1,0:T(1,128)S(1)} all-to-all(s32[8,1,1408]{2,1,0:T(1,128)S(1)} %bitcast.125), channel_id=1, replica_groups=mesh['node'=8,'batch'=4] {'node'}, dimensions={0} | all-to-all | bytes 90112 | tf_op jit(solution)/shard_map/all_to_all | solution.py:114
  43.8 39.8 %gather_fusion = bf16[11264,128]{1,0:T(8,128)(2,1)} fusion(bf16[8192,128]{1,0:T(8,128)(2,1)S(1)} %copy.112, s32[11264]{0:T(1024)S(1)} %broadcast_clamp_fusion), kind=kCustom, calls=%fused_computation | custom fusion | bytes 5812224 | tf_op jit(solution)/shard_map/gather | solution.py:120
  83.7 5.3 %all-to-all-start.1 = ((bf16[8,1408,128]{2,1,0:T(8,128)(2,1)}), bf16[8,1408,128]{2,1,0:T(8,128)(2,1)}, u32[]{:S(2)}, u32[]{:S(2)}) async-start(bf16[8,1408,128]{2,1,0:T(8,128)(2,1)} %bitcast.114), calls=%async_computation.1 | async-start | bytes 5767168 | tf_op jit(solution)/shard_map/all_to_all | solution.py:125
  88.9 1.1 reduce-window.14
  90.5 3.0 scatter_custom_fusion.2
  94.0 0.9 cosine_convert_fusion.1
  94.9 10.1 %cosine_convert_fusion = bf16[512,10,128]{2,0,1:T(8,128)(2,1)} fusion(f32[128]{0:T(128)S(1)} %copy-done.17, f32[128]{0:T(128)S(1)} %copy-done.18, f32[512,10]{0,1:T(8,128)S(1)} %subtract_convert_fusion), kind=kLoop, calls=%fused_computation.20 | loop fusion | flops 1966080 | bytes 1332224 | tf_op jit(solution)/shard_map/convert_element_type | solution.py:170
  105.0 15.5 %all-to-all-done.1 = bf16[8,1408,128]{2,1,0:T(8,128)(2,1)} async-done(((bf16[8,1408,128]{2,1,0:T(8,128)(2,1)}), bf16[8,1408,128]{2,1,0:T(8,128)(2,1)}, u32[]{:S(2)}, u32[]{:S(2)}) %all-to-all-start.1) | async-done | bytes 2883616 | tf_op jit(solution)/shard_map/all_to_all | solution.py:125
  120.5 6.9 %all-to-all-start.3 = ((s32[8,1,128]{2,1,0:T(1,128)}), s32[8,1,128]{2,1,0:T(1,128)S(1)}, u32[]{:S(2)}, u32[]{:S(2)}) async-start(s32[8,1,128]{2,1,0:T(1,128)} %bitcast.18), calls=%async_computation.3 | async-start | bytes 8192 | tf_op jit(solution)/shard_map/all_to_all | solution.py:115
  127.4 13.4 %gather_fusion.1 = bf16[5632,128]{1,0:T(8,128)(2,1)} fusion(bf16[11264,128]{1,0:T(8,128)(2,1)} %bitcast.15, s32[6144]{0:T(1024)S(1)} %pad_clamp_fusion), kind=kCustom, calls=%fused_computation.1 | custom fusion | bytes 2906112 | tf_op jit(solution)/shard_map/gather | solution.py:126
  140.7 3.7 %reshape.238 = bf16[512,11,128]{2,1,0:T(8,128)(2,1)} reshape(bf16[5632,128]{1,0:T(8,128)(2,1)} %gather_fusion.1) | data formatting | bytes 2883584 | tf_op jit(solution)/shard_map/reshape | solution.py:126
  144.4 1.4 slice.78
  145.9 3.2 scatter_custom_fusion.1
  149.0 4.2 %all-to-all-start.2 = ((bf16[8,128,256]{2,1,0:T(8,128)(2,1)}), bf16[8,128,256]{2,1,0:T(8,128)(2,1)S(1)}, u32[]{:S(2)}, u32[]{:S(2)}) async-start(bf16[8,128,256]{2,1,0:T(8,128)(2,1)} %bitcast.16), calls=%async_computation.2 | async-start | bytes 1048576 | tf_op jit(solution)/shard_map/all_to_all | solution.py:137
  153.3 3.2 gather_fusion.2
  156.5 1.5 fusion.65
  158.0 2.6 slice.85
  160.6 1.4 copy.95
  162.4 1.0 copy-done.4
  163.4 1.1 fusion.21
  164.4 4.4 %all-to-all-start.4 = ((bf16[8,128,128]{2,1,0:T(8,128)(2,1)}), bf16[8,128,128]{2,1,0:T(8,128)(2,1)S(1)}, u32[]{:S(2)}, u32[]{:S(2)}) async-start(bf16[8,128,128]{2,1,0:T(8,128)(2,1)} %bitcast.21), calls=%async_computation.4 | async-start | bytes 524288 | tf_op jit(solution)/shard_map/all_to_all | solution.py:145
  168.8 2.6 fusion.4
  171.4 2.3 copy-done.2
  173.7 0.7 all-to-all-done.4
  174.5 1.3 gather_fusion.3
  175.8 1.3 gather_fusion.4
  177.4 4.0 %multiply_reduce_fusion.3 = (f32[512,2,10]{0,1,2:T(2,128)S(1)}, f32[512,10,128]{0,2,1:T(8,128)}) fusion(f32[512,2,64]{0,2,1:T(8,128)S(1)} %bitcast.119, f32[512,10,256]{0,2,1:T(8,128)} %copy-done.2), kind=kLoop, calls=%fused_computation.19 | loop fusion | flops 1300480 | bytes 5545984 | tf_op jit(solution)/shard_map/jvp(ehd,enhd->ehn)/dot_general | solution.py:51
  182.4 1.0 fusion.62
  183.4 0.9 fusion.14
  184.6 2.6 broadcast_multiply_fusion.1
  187.4 0.4 broadcast_multiply_fusion
  187.9 0.9 fusion.15
  189.2 1.6 fusion.11
  190.8 0.7 all-gather.2.cloned.1.call-update
  191.6 10.6 %all_gather.6 = s32[4096]{0:T(1024)S(1)} all-gather(s32[1024]{0:T(1024)S(1)} %get-tuple-element.27), channel_id=1, replica_groups=mesh['node'=8,'batch'=4] {'batch'}, dimensions={0}, use_global_device_ids=true | all-gather | bytes 20480 | tf_op jit(solution)/shard_map/all_gather | solution.py:159
  202.1 26.3 %all-reduce.9.cloned.1.call-done = (f32[128,128]{1,0:T(8,128)}, f32[256,256]{1,0:T(8,128)}, f32[256,128]{1,0:T(8,128)}) async-done(((f32[128,128]{1,0:T(8,128)}, f32[256,256]{1,0:T(8,128)}, f32[256,128]{1,0:T(8,128)}), (f32[128,128]{1,0:T(8,128)}, f32[256,256]{1,0:T(8,128)}, f32[256,128]{1,0:T(8,128)})) %all-reduce.9.cloned.1.call-update) | async-done | bytes 458768 | tf_op jit(solution)/shard_map/psum | solution.py:185
  228.5 24.3 %scatter_custom_fusion.3 = s32[8193]{0:T(1024)S(1)} fusion(s32[4096]{0:T(1024)S(1)} %get-tuple-element.26, s32[4096]{0:T(1024)S(1)} %all_gather.6, s32[]{:T(128)} %constant.30.clone.1), kind=kCustom, calls=%fused_computation.96 | custom fusion | flops 4096 | bytes 32776 | tf_op jit(solution)/shard_map/scatter-max | solution.py:163
  252.8 23.0 %gather_fusion.5 = s32[4096]{0:T(1024)S(1)} fusion(s32[8193]{0:T(1024)S(1)} %scatter_custom_fusion.3, s32[4096]{0:T(1024)S(1)} %get-tuple-element.25), kind=kCustom, calls=%fused_computation.5 | custom fusion | bytes 49152 | tf_op jit(solution)/shard_map/gather | solution.py:164
  275.9 8.2 %psum.62 = f32[128]{0:T(128)S(1)} all-reduce(f32[128]{0:T(128)S(1)} %get-tuple-element.14), channel_id=1, replica_groups=mesh['node'=8,'batch'=4] {'batch'}, use_global_device_ids=true, to_apply=%region_24.25 | all-reduce | flops 128 | bytes 1024 | tf_op jit(solution)/shard_map/psum | solution.py:185
  284.0 17.4 %psum.63 = f32[128]{0:T(128)} all-reduce(f32[128]{0:T(128)S(1)} %psum.62), channel_id=1, replica_groups=mesh['node'=8,'batch'=4] {'node'}, use_global_device_ids=true, to_apply=%region_25.26 | all-reduce | flops 128 | bytes 1024 | tf_op jit(solution)/shard_map/psum | solution.py:186
  301.5 12.5 %scatter_fusion = bf16[8192,128]{1,0:T(8,128)(2,1)S(1)} fusion(bf16[8192,128]{1,0:T(8,128)(2,1)S(1)} %copy.112, s32[4096]{0:T(1024)S(1)} %compare_select_fusion.2, bf16[4096,128]{1,0:T(8,128)(2,1)} %all-gather.2.cloned.1.call-done), kind=kCustom, calls=%fused_computation.10 | custom fusion | bytes 3162112 | tf_op jit(solution)/shard_map/scatter | solution.py:166
  314.0 2.8 all-reduce.7.cloned.1.call-done
  316.8 1.5 copy.113
  318.2 1.7 copy.114
  319.9 1.6 copy.115
  (104 shorter events, 5.7 us)
Async XLA Ops:
  7.2 154.8 %copy-start = (bf16[256,384]{1,0:T(8,128)(2,1)S(1)}, bf16[256,384]{1,0:T(8,128)(2,1)}, u32[]{:S(2)}) copy-start(bf16[256,384]{1,0:T(8,128)(2,1)} %param.28) | copy-start | bytes 589828
  7.2 1.7 copy-start.9
  7.2 5.7 %copy-start.12 = (s32[512,11]{0,1:T(8,128)S(1)}, s32[512,11]{0,1:T(8,128)}, u32[]{:S(2)}) copy-start(s32[512,11]{0,1:T(8,128)} %param.22) | copy-start | bytes 67588
  83.6 5.3 %copy-start.11 = (s32[512,1]{0,1:T(1,128)S(1)}, s32[512,1]{0,1:T(1,128)}, u32[]{:S(2)}) copy-start(s32[512,1]{0,1:T(1,128)} %param.19) | copy-start | bytes 6148
  83.6 6.8 %copy-start.15 = (s32[512]{0:T(512)S(1)}, s32[512]{0:T(512)}, u32[]{:S(2)}) copy-start(s32[512]{0:T(512)} %param.20) | copy-start | bytes 6148
  83.6 10.3 %copy-start.16 = (s32[512]{0:T(512)S(1)}, s32[512]{0:T(512)}, u32[]{:S(2)}) copy-start(s32[512]{0:T(512)} %param.23) | copy-start | bytes 6148
  83.6 10.3 %copy-start.19 = (s32[512]{0:T(512)S(1)}, s32[512]{0:T(512)}, u32[]{:S(2)}) copy-start(s32[512]{0:T(512)} %param.24) | copy-start | bytes 6148
  83.6 10.3 %copy-start.13 = (s32[512,10]{0,1:T(8,128)S(1)}, s32[512,10]{0,1:T(8,128)}, u32[]{:S(2)}) copy-start(s32[512,10]{0,1:T(8,128)} %param.25) | copy-start | bytes 61444
  83.6 10.3 %copy-start.17 = (f32[128]{0:T(128)S(1)}, f32[128]{0:T(128)}, u32[]{:S(2)}) copy-start(f32[128]{0:T(128)} %param.27) | copy-start | bytes 1540
  83.6 10.3 %copy-start.18 = (f32[128]{0:T(128)S(1)}, f32[128]{0:T(128)}, u32[]{:S(2)}) copy-start(f32[128]{0:T(128)} %param.26) | copy-start | bytes 1540
  83.6 43.7 %copy-start.20 = (f32[512]{0:T(512)S(1)}, f32[512]{0:T(512)}, u32[]{:S(2)}) copy-start(f32[512]{0:T(512)} %param.30) | copy-start | bytes 6148
  83.7 36.8 %all-to-all-start.1 = ((bf16[8,1408,128]{2,1,0:T(8,128)(2,1)}), bf16[8,1408,128]{2,1,0:T(8,128)(2,1)}, u32[]{:S(2)}, u32[]{:S(2)}) async-start(bf16[8,1408,128]{2,1,0:T(8,128)(2,1)} %bitcast.114), calls=%async_computation.1 | async-start | bytes 5767168 | tf_op jit(solution)/shard_map/all_to_all | solution.py:125
  120.5 28.5 %all-to-all-start.3 = ((s32[8,1,128]{2,1,0:T(1,128)}), s32[8,1,128]{2,1,0:T(1,128)S(1)}, u32[]{:S(2)}, u32[]{:S(2)}) async-start(s32[8,1,128]{2,1,0:T(1,128)} %bitcast.18), calls=%async_computation.3 | async-start | bytes 8192 | tf_op jit(solution)/shard_map/all_to_all | solution.py:115
  144.4 12.0 %copy-start.8 = (bf16[128,384]{1,0:T(8,128)(2,1)S(1)}, bf16[128,384]{1,0:T(8,128)(2,1)}, u32[]{:S(2)}) copy-start(bf16[128,384]{1,0:T(8,128)(2,1)} %param.29) | copy-start | bytes 294916
  149.0 12.9 %all-to-all-start.2 = ((bf16[8,128,256]{2,1,0:T(8,128)(2,1)}), bf16[8,128,256]{2,1,0:T(8,128)(2,1)S(1)}, u32[]{:S(2)}, u32[]{:S(2)}) async-start(bf16[8,128,256]{2,1,0:T(8,128)(2,1)} %bitcast.16), calls=%async_computation.2 | async-start | bytes 1048576 | tf_op jit(solution)/shard_map/all_to_all | solution.py:137
  162.0 1.4 copy-start.4
  163.4 5.5 %copy-start.7 = (bf16[256,256]{1,0:T(8,128)(2,1)S(1)}, bf16[256,256]{1,0:T(8,128)(2,1)}, u32[]{:S(2)}) copy-start(bf16[256,256]{1,0:T(8,128)(2,1)} %param.32) | copy-start | bytes 393220
  164.4 10.0 %all-to-all-start.4 = ((bf16[8,128,128]{2,1,0:T(8,128)(2,1)}), bf16[8,128,128]{2,1,0:T(8,128)(2,1)S(1)}, u32[]{:S(2)}, u32[]{:S(2)}) async-start(bf16[8,128,128]{2,1,0:T(8,128)(2,1)} %bitcast.21), calls=%async_computation.4 | async-start | bytes 524288 | tf_op jit(solution)/shard_map/all_to_all | solution.py:145
  168.8 59.7 %all-reduce.9.cloned.1.call-start = ((), (), s32[]{:S(2)}) async-start(), calls=%async_computation.7 | async-start | bytes 917504 | tf_op jit(solution)/shard_map/psum | solution.py:185
  171.4 2.3 copy-start.2
  173.7 3.4 %copy-start.14 = (bf16[128,128]{1,0:T(8,128)(2,1)S(1)}, bf16[128,128]{1,0:T(8,128)(2,1)}, u32[]{:S(2)}) copy-start(bf16[128,128]{1,0:T(8,128)(2,1)} %param.31) | copy-start | bytes 98308
  177.4 4.2 %slice-start = ((f32[512,10,256]{0,2,1:T(8,128)}), f32[512,10,128]{0,2,1:T(8,128)S(1)}, s32[]{:S(2)}) async-start(f32[512,10,256]{0,2,1:T(8,128)} %copy-done.2), calls=%async_computation.8 | async-start | bytes 5242880 | tf_op jit(solution)/shard_map/jvp()/slice | solution.py:50
  181.4 0.8 copy-start.10
  181.4 1.0 copy-start.21
  181.4 1.0 copy-start.22
  184.6 2.8 copy-start.3
  187.4 1.3 copy-start.5
  187.4 1.7 copy-start.6
  190.8 110.7 %all-gather.2.cloned.1.call-start = ((), (), s32[]{:S(2)}) async-start(), calls=%async_computation.5 | async-start | bytes 1310720 | tf_op jit(solution)/shard_map/all_gather | solution.py:158
  191.5 125.2 %all-reduce.7.cloned.1.call-start = ((), (), s32[]{:S(2)}) async-start(), calls=%async_computation.6 | async-start | bytes 917504 | tf_op jit(solution)/shard_map/psum | solution.py:186
  313.9 7.5 %copy-start.1 = (bf16[8192,128]{1,0:T(8,128)(2,1)}, bf16[8192,128]{1,0:T(8,128)(2,1)S(1)}, u32[]{:S(2)}) copy-start(bf16[8192,128]{1,0:T(8,128)(2,1)S(1)} %scatter_fusion) | copy-start | bytes 6291460
Sparse Core Ops, SparseCore 0:
  190.9 37.5 all-reduce.8
  230.7 28.5 all-gather.1
  263.0 53.6 all-reduce.6
